TPU v7x, 128 devices: a whole 4x4x4 slice. The times are simulated.
128 devices in a mesh: wide: 16 (over y_lo, z, core), narrow: 8 (over y_hi, x).
Axes of the slice: x: 4, y: 4 (y_hi: 2, y_lo: 2; y = y_hi * 2 + y_lo), z: 4, core: 2. Of those that a mesh axis runs over, the one named last changes fastest.
Arguments:
- vit_tokens: bfloat16 [1024, 6144], P('wide', 'narrow'), may hold values from -18 to 18
- ln_gain: float32 [6144], P('narrow'), may hold values from 0.25 to 1.75
- w_fc1: bfloat16 [6144, 12288], P('narrow', 'wide'), may hold values from -0.078125 to 0.078125
- b_fc1: float32 [12288], P('wide'), may hold values from -3 to 3
- w_fc2: bfloat16 [12288, 6144], P('wide', 'narrow'), may hold values from -0.0546875 to 0.0546875
- b_fc2: float32 [6144], P('narrow'), may hold values from -3 to 3
- w_proj: bfloat16 [6144, 4096], P('narrow', 'wide'), may hold values from -0.078125 to 0.078125
- b_proj: float32 [4096], replicated, may hold values from -3 to 3
- text_states: bfloat16 [7168, 4096], P(('wide', 'narrow')), may hold values from -10 to 10
- rms_gain: float32 [4096], replicated, may hold values from 0.25 to 1.75
- w_gate: bfloat16 [4096, 8192], P('wide', 'narrow'), may hold values from -0.09375 to 0.09375
- w_up: bfloat16 [4096, 8192], P('wide', 'narrow'), may hold values from -0.09375 to 0.09375
- w_out: bfloat16 [8192, 4096], P('narrow', 'wide'), may hold values from -0.0625 to 0.0625
Outputs:
- vit_out: bfloat16 [1024, 6144], P('wide', 'narrow')
- ul2_image: bfloat16 [1024, 4096], P(('wide', 'narrow'))
- ul2_text: bfloat16 [7168, 4096], P(('wide', 'narrow'))
All inputs are finite; a program needn't handle non-finite values.
Results may differ from a plain program's by a relative error of at most 0.03.
Values may be sent and summed in bfloat16 or wider, within the bound.
A program may use at most 128 MiB of HBM per device.

v0:
```python
import jax
import jax.numpy as jnp
from jax import lax
from jax.sharding import PartitionSpec as P

DV = 6144


def on_device(
    vit_tokens,
    ln_gain,
    w_fc1,
    b_fc1,
    w_fc2,
    b_fc2,
    w_proj,
    b_proj,
    text_states,
    rms_gain,
    w_gate,
    w_up,
    w_out,
):
    tokens = vit_tokens.astype(jnp.float32)
    sums, squares = lax.psum((jnp.sum(tokens, -1), jnp.sum(tokens * tokens, -1)), "narrow")
    mean = sums / DV
    variance = squares / DV - mean * mean
    scale = lax.rsqrt(variance + 1e-06)
    ln_rows = ((tokens - mean[:, None]) * scale[:, None] * ln_gain).astype(jnp.bfloat16)
    rows_all = lax.all_gather(ln_rows, "wide", axis=0, tiled=True)
    block = rows_all
    fc1_sum = lax.psum_scatter(
        jnp.dot(block, w_fc1, preferred_element_type=jnp.float32).astype(jnp.bfloat16),
        "narrow",
        scatter_dimension=0,
        tiled=True,
    ).astype(jnp.float32)
    hidden = jax.nn.gelu(fc1_sum + b_fc1, approximate=False).astype(jnp.bfloat16)
    hidden_all = lax.all_gather(hidden, "narrow", axis=0, tiled=True)
    block = hidden_all
    fc2_sum = lax.psum_scatter(
        jnp.dot(block, w_fc2, preferred_element_type=jnp.float32).astype(jnp.bfloat16),
        "wide",
        scatter_dimension=0,
        tiled=True,
    ).astype(jnp.float32)
    vit_out = (tokens + fc2_sum + b_fc2).astype(jnp.bfloat16)
    partial_proj = jnp.dot(
        vit_out,
        lax.all_gather(w_proj, "wide", axis=1, tiled=True),
        preferred_element_type=jnp.float32,
    )
    proj_sum = lax.psum_scatter(
        partial_proj.astype(jnp.bfloat16), "narrow", scatter_dimension=0, tiled=True
    ).astype(jnp.float32)
    image_states = (proj_sum + b_proj).astype(jnp.bfloat16)
    image_count = image_states.shape[0]
    states = jnp.concatenate([image_states, text_states], 0).astype(jnp.float32)
    rms_scale = lax.rsqrt(jnp.mean(states * states, -1, keepdims=True) + 1e-06)
    rms_rows = (states * rms_scale * rms_gain).astype(jnp.bfloat16)
    group_rows = lax.all_gather(rms_rows, "narrow", axis=0, tiled=True)
    gate = jnp.dot(
        group_rows,
        lax.all_gather(w_gate, "wide", axis=0, tiled=True),
        preferred_element_type=jnp.float32,
    )
    up_part = jnp.dot(
        group_rows,
        lax.all_gather(w_up, "wide", axis=0, tiled=True),
        preferred_element_type=jnp.float32,
    )
    inner = (jax.nn.silu(gate) * up_part).astype(jnp.bfloat16)
    partial_out = jnp.dot(
        inner, lax.all_gather(w_out, "wide", axis=1, tiled=True), preferred_element_type=jnp.float32
    )
    out_sum = lax.psum_scatter(
        partial_out.astype(jnp.bfloat16), "narrow", scatter_dimension=0, tiled=True
    ).astype(jnp.float32)
    result = (states + out_sum).astype(jnp.bfloat16)
    return (vit_out, result[:image_count], result[image_count:])


def solution(mesh):
    return jax.shard_map(
        on_device,
        mesh=mesh,
        in_specs=(
            P("wide", "narrow"),
            P("narrow"),
            P("narrow", "wide"),
            P("wide"),
            P("wide", "narrow"),
            P("narrow"),
            P("narrow", "wide"),
            P(),
            P(("wide", "narrow"), None),
            P(),
            P("wide", "narrow"),
            P("wide", "narrow"),
            P("narrow", "wide"),
        ),
        out_specs=(P("wide", "narrow"), P(("wide", "narrow"), None), P(("wide", "narrow"), None)),
        check_vma=False,
    )
```

profile of v0, /device:TPU:1, one launch (start us, length us, event | category | flops | bytes accessed | tf_op | source)
XLA Modules:
  0.0 744.0 jit_solution(16807698032464398688)
XLA Ops:
  7.2 1.1 convert_reduce_fusion
  8.3 21.4 %all-reduce = (f32[64]{0:T(128)S(1)}, f32[64]{0:T(128)S(1)}) all-reduce(f32[64]{0:T(128)S(1)} %get-tuple-element.4, f32[64]{0:T(128)S(1)} %get-tuple-element.3), channel_id=1, replica_groups=mesh['wide'=16,'narrow'=8] {'narrow'}, use_global_device_ids=true, to_apply=%region_3.0 | all-reduce | flops 128 | bytes 1024 | tf_op jit(solution)/shard_map/psum | solution.py:25
  29.8 1.6 fusion.19
  31.5 35.3 %all-gather.8.cloned.1.call-done = bf16[1024,768]{1,0:T(8,128)(2,1)} async-done(((bf16[64,768]{1,0:T(8,128)(2,1)}), bf16[1024,768]{1,0:T(8,128)(2,1)}) %all-gather.8.cloned.1.call-update) | async-done | bytes 1572880 | tf_op jit(solution)/shard_map/all_gather | solution.py:30
  66.8 4.0 convolution_convert_fusion.3
  70.9 72.8 %reduce-scatter.5.cloned.1.call-done = bf16[128,768]{1,0:T(8,128)(2,1)} async-done(((bf16[1024,768]{1,0:T(8,128)(2,1)}), bf16[128,768]{1,0:T(8,128)(2,1)}) %reduce-scatter.5.cloned.1.call-update) | async-done | bytes 196624 | tf_op jit(solution)/shard_map/reduce_scatter | solution.py:32
  143.7 2.5 fusion.6
  146.3 50.0 %all-gather.10.cloned.1.call-done = bf16[1024,768]{1,0:T(8,128)(2,1)} async-done(((bf16[128,768]{1,0:T(8,128)(2,1)}), bf16[1024,768]{1,0:T(8,128)(2,1)}) %all-gather.10.cloned.1.call-update) | async-done | bytes 1572880 | tf_op jit(solution)/shard_map/all_gather | solution.py:39
  196.3 3.9 convolution_convert_fusion.2
  200.3 0.5 all-gather.12.cloned.1.call-update
  200.9 58.6 %reduce-scatter.7.cloned.1.call-done = bf16[64,768]{1,0:T(8,128)(2,1)} async-done(((bf16[1024,768]{1,0:T(8,128)(2,1)}), bf16[64,768]{1,0:T(8,128)(2,1)}) %reduce-scatter.7.cloned.1.call-update) | async-done | bytes 98320 | tf_op jit(solution)/shard_map/reduce_scatter | solution.py:41
  259.4 0.9 fusion.22
  260.4 56.4 %all-gather.12.cloned.1.call-done = bf16[768,4096]{1,0:T(8,128)(2,1)} async-done(((bf16[768,256]{1,0:T(8,128)(2,1)}), bf16[768,4096]{1,0:T(8,128)(2,1)}) %all-gather.12.cloned.1.call-update) | async-done | bytes 6291472 | tf_op jit(solution)/shard_map/all_gather | solution.py:50
  316.8 4.8 convolution_convert_fusion.1
  321.7 0.7 all-gather.16.cloned.1.call-update
  322.5 67.0 %reduce-scatter.9.cloned.1.call-done = bf16[8,4096]{1,0:T(8,128)(2,1)} async-done(((bf16[64,4096]{1,0:T(8,128)(2,1)}), bf16[8,4096]{1,0:T(8,128)(2,1)}) %reduce-scatter.9.cloned.1.call-update) | async-done | bytes 65552 | tf_op jit(solution)/shard_map/reduce_scatter | solution.py:53
  389.5 0.9 add_convert_fusion
  390.3 0.2 fusion
  390.5 1.0 fusion.2
  391.7 0.7 all-gather.18.cloned.1.call-update
  392.4 0.5 all-gather.20.cloned.1.call-update
  392.9 0.2 reduce-scatter.11.cloned.1.call-start
  393.2 51.6 %all-gather.16.cloned.1.call-done = bf16[4096,1024]{1,0:T(8,128)(2,1)} async-done(((bf16[256,1024]{1,0:T(8,128)(2,1)}), bf16[4096,1024]{1,0:T(8,128)(2,1)}) %all-gather.16.cloned.1.call-update) | async-done | bytes 8388624 | tf_op jit(solution)/shard_map/all_gather | solution.py:64
  444.8 74.0 %all-gather.14.cloned.1.call-done = bf16[512,4096]{1,0:T(8,128)(2,1)} async-done(((bf16[64,4096]{1,0:T(8,128)(2,1)}), bf16[512,4096]{1,0:T(8,128)(2,1)}) %all-gather.14.cloned.1.call-update) | async-done | bytes 4194320 | tf_op jit(solution)/shard_map/all_gather | solution.py:61
  518.8 10.5 %fusion.23 = f32[512,1024]{1,0:T(8,128)} fusion(bf16[512,4096]{1,0:T(8,128)(2,1)} %all-gather.14.cloned.1.call-done, bf16[4096,1024]{1,0:T(8,128)(2,1)} %all-gather.16.cloned.1.call-done), kind=kOutput, calls=%fused_computation.49 | convolution fusion | flops 4294967296 | bytes 14680064 | tf_op jit(solution)/shard_map/dot_general | solution.py:62
  529.3 42.2 %all-gather.18.cloned.1.call-done = bf16[4096,1024]{1,0:T(8,128)(2,1)} async-done(((bf16[256,1024]{1,0:T(8,128)(2,1)}), bf16[4096,1024]{1,0:T(8,128)(2,1)}) %all-gather.18.cloned.1.call-update) | async-done | bytes 8388624 | tf_op jit(solution)/shard_map/all_gather | solution.py:69
  571.4 63.3 %all-gather.20.cloned.1.call-done = bf16[1024,4096]{1,0:T(8,128)(2,1)} async-done(((bf16[1024,256]{1,0:T(8,128)(2,1)}), bf16[1024,4096]{1,0:T(8,128)(2,1)}) %all-gather.20.cloned.1.call-update) | async-done | bytes 8388624 | tf_op jit(solution)/shard_map/all_gather | solution.py:74
  634.7 17.3 %convolution_convert_fusion = bf16[512,4096]{1,0:T(8,128)(2,1)} fusion(bf16[1024,4096]{1,0:T(8,128)(2,1)} %all-gather.20.cloned.1.call-done, f32[512,1024]{1,0:T(8,128)} %fusion.23, bf16[512,4096]{1,0:T(8,128)(2,1)} %all-gather.14.cloned.1.call-done, bf16[4096,1024]{1,0:T(8,128)(2,1)} %all-gather.18.cloned.1.call-done), kind=kOutput, calls=%fused_computation | convolution fusion | flops 8595177472 | bytes 27262976 | tf_op jit(solution)/shard_map/dot_general | solution.py:73
  652.1 82.9 %reduce-scatter.11.cloned.1.call-done = bf16[64,4096]{1,0:T(8,128)(2,1)} async-done(((bf16[512,4096]{1,0:T(8,128)(2,1)}), bf16[64,4096]{1,0:T(8,128)(2,1)}) %reduce-scatter.11.cloned.1.call-update) | async-done | bytes 524304 | tf_op jit(solution)/shard_map/reduce_scatter | solution.py:76
  734.9 1.2 fusion.3
  736.1 0.8 slice.9
  736.9 0.6 slice.8
  (37 shorter events, 0.6 us)
Async XLA Ops:
  7.2 59.7 %copy-start = (bf16[768,768]{1,0:T(8,128)(2,1)S(1)}, bf16[768,768]{1,0:T(8,128)(2,1)}, u32[]{:S(2)}) copy-start(bf16[768,768]{1,0:T(8,128)(2,1)} %param.15) | copy-start | bytes 3538948
  7.2 59.6 %all-gather.8.cloned.1.call-start = ((), (), s32[]{:S(2)}) async-start(), calls=%async_computation.4 | async-start | bytes 1671168 | tf_op jit(solution)/shard_map/all_gather | solution.py:30
  31.4 112.3 %copy-start.6 = (f32[768]{0:T(1024)S(1)}, f32[768]{0:T(1024)}, u32[]{:S(2)}) copy-start(f32[768]{0:T(1024)} %param.16) | copy-start | bytes 9220
  31.4 112.3 %reduce-scatter.5.cloned.1.call-start = ((), (), s32[]{:S(2)}) async-start(), calls=%async_computation.5 | async-start | bytes 1769472 | tf_op jit(solution)/shard_map/reduce_scatter | solution.py:32
  70.8 125.5 %copy-start.8 = (bf16[768,768]{1,0:T(8,128)(2,1)S(1)}, bf16[768,768]{1,0:T(8,128)(2,1)}, u32[]{:S(2)}) copy-start(bf16[768,768]{1,0:T(8,128)(2,1)} %param.17) | copy-start | bytes 3538948
  70.8 125.4 %all-gather.10.cloned.1.call-start = ((), (), s32[]{:S(2)}) async-start(), calls=%async_computation.6 | async-start | bytes 1769472 | tf_op jit(solution)/shard_map/all_gather | solution.py:39
  146.2 113.2 %copy-start.2 = (bf16[64,768]{1,0:T(8,128)(2,1)S(1)}, bf16[64,768]{1,0:T(8,128)(2,1)}, u32[]{:S(2)}) copy-start(bf16[64,768]{1,0:T(8,128)(2,1)} %param.13) | copy-start | bytes 294916
  146.2 113.2 %copy-start.7 = (f32[768]{0:T(1024)S(1)}, f32[768]{0:T(1024)}, u32[]{:S(2)}) copy-start(f32[768]{0:T(1024)} %param.18) | copy-start | bytes 9220
  146.2 113.2 %reduce-scatter.7.cloned.1.call-start = ((), (), s32[]{:S(2)}) async-start(), calls=%async_computation.7 | async-start | bytes 1671168 | tf_op jit(solution)/shard_map/reduce_scatter | solution.py:41
  200.2 116.6 %all-gather.12.cloned.1.call-start = ((), (), s32[]{:S(2)}) async-start(), calls=%async_computation.8 | async-start | bytes 6684672 | tf_op jit(solution)/shard_map/all_gather | solution.py:50
  200.8 188.6 %reduce-scatter.9.cloned.1.call-start = ((), (), s32[]{:S(2)}) async-start(), calls=%async_computation.9 | async-start | bytes 589824 | tf_op jit(solution)/shard_map/reduce_scatter | solution.py:53
  260.4 61.3 %copy-start.3 = (bf16[64,768]{1,0:T(8,128)(2,1)}, bf16[64,768]{1,0:T(8,128)(2,1)S(1)}, u32[]{:S(2)}) copy-start(bf16[64,768]{1,0:T(8,128)(2,1)S(1)} %fusion.22) | copy-start | bytes 294916
  260.4 129.1 %copy-start.5 = (f32[4096]{0:T(1024)S(1)}, f32[4096]{0:T(1024)}, u32[]{:S(2)}) copy-start(f32[4096]{0:T(1024)} %param.20) | copy-start | bytes 49156
  260.4 129.9 %copy-start.1 = (bf16[56,4096]{1,0:T(8,128)(2,1)S(1)}, bf16[56,4096]{1,0:T(8,128)(2,1)}, u32[]{:S(2)}) copy-start(bf16[56,4096]{1,0:T(8,128)(2,1)} %param.21) | copy-start | bytes 1376260
  260.4 130.2 %copy-start.4 = (f32[4096]{0:T(1024)S(1)}, f32[4096]{0:T(1024)}, u32[]{:S(2)}) copy-start(f32[4096]{0:T(1024)} %param.22) | copy-start | bytes 49156
  321.7 123.1 %all-gather.16.cloned.1.call-start = ((), (), s32[]{:S(2)}) async-start(), calls=%async_computation.11 | async-start | bytes 8912896 | tf_op jit(solution)/shard_map/all_gather | solution.py:64
  322.4 196.3 %all-gather.14.cloned.1.call-start = ((), (), s32[]{:S(2)}) async-start(), calls=%async_computation.10 | async-start | bytes 4718592 | tf_op jit(solution)/shard_map/all_gather | solution.py:61
  391.6 179.8 %all-gather.18.cloned.1.call-start = ((), (), s32[]{:S(2)}) async-start(), calls=%async_computation.12 | async-start | bytes 8912896 | tf_op jit(solution)/shard_map/all_gather | solution.py:69
  392.4 242.4 %all-gather.20.cloned.1.call-start = ((), (), s32[]{:S(2)}) async-start(), calls=%async_computation.13 | async-start | bytes 8912896 | tf_op jit(solution)/shard_map/all_gather | solution.py:74
  392.9 342.0 %reduce-scatter.11.cloned.1.call-start = ((), (), s32[]{:S(2)}) async-start(), calls=%async_computation.14 | async-start | bytes 4718592 | tf_op jit(solution)/shard_map/reduce_scatter | solution.py:76
Sparse Core Ops, SparseCore 0:
  31.5 35.2 all-gather.7
  70.9 72.7 reduce-scatter.4
  146.6 49.6 all-gather.9
  200.3 59.0 reduce-scatter.6
  261.0 55.7 all-gather.11
  321.8 67.6 reduce-scatter.8
  391.2 53.5 all-gather.15
  447.1 71.6 all-gather.13
  520.5 50.9 all-gather.17
  572.9 61.7 all-gather.19
  652.2 82.6 reduce-scatter.10
where the time goes:
time: 745 us; the launch traced here: 744 us
  waiting for transfers between devices  657 us (88%)
  matrix products  40.5 us (5%)
  blocking collectives  21.4 us (3%)
  between operations  14 us (2%)
  other arithmetic  9.42 us (1%)
    reduce_scatter x1, waiting for transfers between devices, on_device(): lax.psum_scatter(partial_out.astype(jnp.bfloat16), 'narrow', scatter_dime...  82.9 us
    all_gather x1, waiting for transfers between devices, on_device(): group_rows = lax.all_gather(rms_rows, 'narrow', axis=0, tiled=True)  74 us
    reduce_scatter x1, waiting for transfers between devices, on_device(): lax.psum_scatter(jnp.dot(block, w_fc1, preferred_element_type=jnp.float32...  72.8 us
    reduce_scatter x1, waiting for transfers between devices, on_device(): lax.psum_scatter(partial_proj.astype(jnp.bfloat16), 'narrow', scatter_dim...  67 us
    all_gather x1, waiting for transfers between devices, on_device(): lax.all_gather(w_out, 'wide', axis=1, tiled=True)  63.3 us
    reduce_scatter x1, waiting for transfers between devices, on_device(): lax.psum_scatter(jnp.dot(block, w_fc2, preferred_element_type=jnp.float32...  58.6 us
    all_gather x1, waiting for transfers between devices, on_device(): lax.all_gather(w_proj, 'wide', axis=1, tiled=True)  56.4 us
    all_gather x1, waiting for transfers between devices, on_device(): lax.all_gather(w_gate, 'wide', axis=0, tiled=True)  51.6 us
  transfers between devices with their start and end apart: 11, of which 11 were waited for; matrix products, arithmetic and copies ran while one was open for 2% of the time, Pallas kernels for 0%

commit v1 on v0

v1 whole, which is shorter than its diff:
```python
import jax
import jax.numpy as jnp
from jax import lax
from jax.experimental import pallas as pl
from jax.experimental.pallas import tpu as pltpu
from jax.sharding import PartitionSpec as P

DV = 6144
DU = 4096
F32 = jnp.float32
BF16 = jnp.bfloat16
MESH = pl.DeviceIdType.MESH
EARLY = 48
LATE = 16
REST = [(0, 1), (0, 3), (1, 0), (0, 2), (1, 1), (1, 3), (1, 2)]
PLACES = [(0, 0)] + REST
ORDER = [(0, 0), (0, 3), (0, 1), (1, 0), (0, 2), (1, 3), (1, 1), (1, 2)]
R03, R01, R10, R02L, R02U, R13, R11, R12L, R12U, RSIB = range(10)


def dot(a, b):
    return jnp.dot(a, b, preferred_element_type=F32)


class Gather:
    def __init__(self, own, slot, half, dev, sib, send_sem, recv_sem, sends, local_sem=None):
        self.own, self.slot, self.half, self.dev, self.sib = own, slot, half, dev, sib
        self.send_sem, self.recv_sem, self.sends, self.count = send_sem, recv_sem, sends, 0
        self.local_sem = local_sem

    def send(self, src, dst, to, sem):
        copy = pltpu.make_async_remote_copy(
            src_ref=src,
            dst_ref=dst,
            send_sem=self.send_sem.at[self.count],
            recv_sem=self.recv_sem.at[sem],
            device_id=to,
            device_id_type=MESH,
        )
        copy.start()
        self.count += 1
        self.sends.append(copy)

    def wait(self, ref, sem):
        pltpu.make_async_remote_copy(
            src_ref=ref,
            dst_ref=ref,
            send_sem=self.send_sem.at[0],
            recv_sem=self.recv_sem.at[sem],
            device_id=self.dev(0, 1),
            device_id_type=MESH,
        ).wait_recv()

    def share(self, place, src=None):
        if self.sib is not None:
            ref = self.slot(*place, 0)
            self.send(ref if src is None else src, ref, self.sib, RSIB + PLACES.index(place))

    def begin(self):
        mine = self.slot(0, 0, 0)
        self.send(self.own, mine, self.dev(1, 0), R10)
        self.send(self.own, mine, self.dev(0, 1), R03)
        self.send(self.own, mine, self.dev(0, 3), R01)
        self.share((0, 0), self.own)
        if self.local_sem is not None:
            pltpu.make_async_copy(self.own, mine, self.local_sem).start()

    def forward(self, place, low, sem):
        ref = self.half(self.slot(*place, 0), 0 if low else 1)
        self.send(ref, ref, self.dev(0, 1 if low else 3), sem)

    def event(self, e):
        slot, half = self.slot, self.half
        if e == 1:
            self.wait(slot(0, 3, 0), R03)
            self.forward((0, 3), True, R02L)
            self.share((0, 3))
        elif e == 2:
            self.wait(slot(0, 1, 0), R01)
            self.forward((0, 1), False, R02U)
            self.share((0, 1))
        elif e == 3:
            ref = slot(1, 0, 0)
            self.wait(ref, R10)
            self.send(ref, ref, self.dev(0, 1), R13)
            self.send(ref, ref, self.dev(0, 3), R11)
            self.share((1, 0))
        elif e == 4:
            self.wait(half(slot(0, 2, 0), 0), R02L)
            self.wait(half(slot(0, 2, 0), 1), R02U)
            self.share((0, 2))
        elif e == 5:
            self.wait(slot(1, 3, 0), R13)
            self.forward((1, 3), True, R12L)
            self.share((1, 3))
        elif e == 6:
            self.wait(slot(1, 1, 0), R11)
            self.forward((1, 1), False, R12U)
            self.share((1, 1))
        else:
            self.wait(half(slot(1, 2, 0), 0), R12L)
            self.wait(half(slot(1, 2, 0), 1), R12U)
            self.share((1, 2))

    def wait_sibling(self, place):
        self.wait(self.slot(*place, 1), RSIB + PLACES.index(place))

    def wait_local(self):
        pltpu.make_async_copy(self.own, self.slot(0, 0, 0), self.local_sem).wait()

    def wait_siblings(self):
        self.wait_local()
        for place in ORDER:
            self.wait_sibling(place)


def kernel(
    vit_ref, ln_gain_ref, wfc1_ref, b1_ref, wfc2_ref, b2_ref, wproj_ref, bproj_ref,
    text_ref, rms_gain_ref, wgate_ref, wup_ref, wout_ref,
    vout_ref, res_ref,
    wg, wu, wo, wp,
    stat, xg, part, rs1, hg, sib2, rs2, pp, rp,
    re, rl, gacc, inner, inner_l, oe, rx, ys, yr, ol, ro, img,
    wss, wrs, tss, trs, lsem, dss, drs,
):
    w, n = lax.axis_index("wide"), lax.axis_index("narrow")
    c, z, yl = lax.rem(w, 2), lax.rem(w // 2, 4), w // 8
    x, yh = lax.rem(n, 4), n // 4

    def chip(dy, dz):
        return lax.rem(yl + dy, 2) * 4 + lax.rem(z + dz, 4)

    def wide_dev(dy, dz):
        return (chip(dy, dz) * 2 + c, n)

    def near(dy, dx):
        return lax.rem(yh + dy, 2) * 4 + lax.rem(x + dx, 4)

    def narrow_dev(dy, dx):
        return (w, near(dy, dx))

    sib = (chip(0, 0) * 2 + 1 - c, n)

    barrier = pltpu.get_barrier_semaphore()
    peers = [sib] + [wide_dev(*p) for p in REST] + [narrow_dev(*p) for p in REST]
    for peer in peers:
        pl.semaphore_signal(barrier, inc=1, device_id=peer, device_id_type=MESH)
    pl.semaphore_wait(barrier, len(peers))

    sends = []
    used = [0]

    def back(place):
        return (place[0], (4 - place[1]) % 4)

    def index(place):
        return REST.index(place)

    def send(src, dst, to, sem, keep=True):
        copy = pltpu.make_async_remote_copy(
            src_ref=src, dst_ref=dst, send_sem=dss.at[used[0]], recv_sem=drs.at[sem],
            device_id=to, device_id_type=MESH,
        )
        used[0] += 1
        copy.start()
        if keep:
            sends.append(copy)
        return copy

    def wait(ref, sem):
        pltpu.make_async_remote_copy(
            src_ref=ref, dst_ref=ref, send_sem=dss.at[0], recv_sem=drs.at[sem],
            device_id=sib, device_id_type=MESH,
        ).wait_recv()

    STAT, X, XSIB, RS1, HID, COMB, RS2, PROJ, LATE_IN, LATE_OUT, RX, RY = 0, 7, 14, 22, 36, 50, 52, 59, 66, 73, 80, 104

    def rows_of(buf, rows):
        def slot(dy, dz, other):
            start = (chip(dy, dz) * 2 + (1 - c if other else c)) * rows
            return buf.at[pl.ds(pl.multiple_of(start, rows), rows)]
        return slot

    def halves(rows):
        return lambda ref, k: ref.at[pl.ds(k * rows // 2, rows // 2)]

    def gather(i, own, buf, rows):
        return Gather(own, rows_of(buf, rows), halves(rows), wide_dev, sib, wss.at[i], wrs.at[i], sends, lsem.at[i])

    gate_g = gather(0, wgate_ref, wg, 256)
    up_g = gather(1, wup_ref, wu, 256)
    out_g = gather(2, wout_ref, wo, 1024)
    proj_g = gather(3, wproj_ref, wp, 768)

    def text_slot(dy, dx, other):
        return re.at[near(dy, dx)]

    text_g = Gather(
        re.at[n], text_slot, lambda ref, k: ref.at[:, pl.ds(k * DU // 2, DU // 2)],
        narrow_dev, None, tss, trs, sends,
    )

    def stats():
        rows = vit_ref[...].astype(F32)
        total = jnp.sum(rows, -1, keepdims=True)
        square = jnp.sum(rows * rows, -1, keepdims=True)
        lane = lax.broadcasted_iota(jnp.int32, (64, 128), 1)
        both = jnp.where(lane == 0, total, jnp.where(lane == 1, square, 0.0))
        turned = jnp.transpose(jnp.concatenate([both, jnp.zeros_like(both)], 0))
        stat[n] = turned[0:8]
        for p in REST:
            send(stat.at[n], stat.at[n], narrow_dev(*p), STAT + index(back(p)))

    def text_rows():
        rows = text_ref[...].astype(F32)
        scale = lax.rsqrt(jnp.mean(rows * rows, -1, keepdims=True) + 1e-06)
        normed = rows * scale * rms_gain_ref[...]
        re[n] = normed[0:EARLY].astype(BF16)

    def layer_norm():
        for p in REST:
            wait(stat.at[near(*p)], STAT + index(p))
        total = stat[0]
        for k in range(1, 8):
            total = total + stat[k]
        turned = jnp.transpose(jnp.concatenate([total, jnp.zeros((120, 128), F32)], 0))
        mean = turned[0:64, 0:1] / DV
        variance = turned[0:64, 1:2] / DV - mean * mean
        scale = lax.rsqrt(variance + 1e-06)
        rows = vit_ref[...].astype(F32)
        xg[w] = ((rows - mean) * scale * ln_gain_ref[...]).astype(BF16)
        for p in REST:
            send(xg.at[w], xg.at[w], wide_dev(*p), X + index(back(p)))
        send(xg.at[w], xg.at[w], sib, XSIB)

    def x_arrivals(h):
        order = [p for p in REST if p[0] == h]
        for p in order:
            ref = xg.at[chip(*p) * 2 + c]
            wait(ref, X + index(p))
            send(ref, ref, sib, XSIB + 1 + index(p))
        for p in PLACES:
            if p[0] == h:
                wait(xg.at[chip(*p) * 2 + 1 - c], XSIB + PLACES.index(p))

    def half_start(h):
        return lax.rem(yl + h, 2) * 4

    rs1_sends = {0: [], 1: []}

    def fc1(h):
        def step(i, carry):
            first = half_start(h) + 2 * i
            rows = xg[pl.ds(first * 2, 4)].reshape(256, 768)
            out = dot(rows, wfc1_ref[...]).astype(BF16).reshape(2, 8, 16, 768)
            part[:, first] = out[0]
            part[:, first + 1] = out[1]
            return carry
        lax.fori_loop(0, 2, step, 0)
        chips = pl.ds(half_start(h), 4)
        for p in REST:
            rs1_sends[h].append(
                send(part.at[near(*p), chips], rs1.at[n, chips], narrow_dev(*p), RS1 + 7 * h + index(back(p)), False)
            )

    def gelu(h):
        chips = pl.ds(half_start(h), 4)
        total = part[n, chips].astype(F32)
        for p in REST:
            wait(rs1.at[near(*p), chips], RS1 + 7 * h + index(p))
            total = total + rs1[near(*p), chips].astype(F32)
        v = total.reshape(64, 768) + b1_ref[...]
        hidden = 0.5 * v * (1.0 + lax.erf(v * (0.5 ** 0.5)))
        hg[n, chips] = hidden.astype(BF16).reshape(4, 16, 768)
        for p in REST:
            send(hg.at[n, chips], hg.at[n, chips], narrow_dev(*p), HID + 7 * h + index(back(p)))

    def fc2(h):
        chips = pl.ds(half_start(h), 4)
        for p in REST:
            wait(hg.at[near(*p), chips], HID + 7 * h + index(p))
        for copy in rs1_sends[h]:
            copy.wait_send()

        def step(i, carry):
            two = pl.ds(half_start(h) + 2 * i, 2)
            rows = hg[:, two].reshape(256, 768)
            part[:, two] = dot(rows, wfc2_ref[...]).astype(BF16).reshape(8, 2, 16, 768)
            return carry
        lax.fori_loop(0, 2, step, 0)
        send(part.at[pl.ds(4 * (1 - c), 4), chips], sib2.at[:, chips], sib, COMB + h)

    def combine(h):
        chips = pl.ds(half_start(h), 4)
        wait(sib2.at[:, chips], COMB + h)
        mine = part[pl.ds(4 * c, 4), chips].astype(F32)
        sib2[:, chips] = (mine + sib2[:, chips].astype(F32)).astype(BF16)
        for p in REST:
            if p[0] == h:
                send(sib2.at[:, chip(*p)], rs2.at[chip(0, 0)], wide_dev(*p), RS2 + index(back(p)))

    def vit_out():
        total = sib2[:, chip(0, 0)].astype(F32)
        for p in REST:
            wait(rs2.at[chip(*p)], RS2 + index(p))
            total = total + rs2[chip(*p)].astype(F32)
        rows = vit_ref[...].astype(F32) + total.reshape(64, 768) + b2_ref[...]
        vout_ref[...] = rows.astype(BF16)

    def proj():
        proj_g.wait_siblings()

        def step(i, carry):
            rows = vout_ref[...]
            low = dot(rows, wp[pl.ds(pl.multiple_of(i * 768, 768), 768)]).reshape(8, 8, 256)
            high = dot(rows, wp[pl.ds(pl.multiple_of((i + 8) * 768, 768), 768)]).reshape(8, 8, 256)
            pp[:, :, pl.ds(pl.multiple_of(i * 256, 256), 256)] = jnp.concatenate([low, high], 1).astype(BF16)
            return carry
        lax.fori_loop(0, 8, step, 0)
        for p in REST:
            send(pp.at[near(*p)], rp.at[n], narrow_dev(*p), PROJ + index(back(p)))

    def image_rows():
        total = pp[n].astype(F32)
        for p in REST:
            wait(rp.at[near(*p)], PROJ + index(p))
            total = total + rp[near(*p)].astype(F32)
        rows = jnp.concatenate([total[0:8], total[8:16]], 1) + bproj_ref[...]
        image = rows.astype(BF16).astype(F32)
        late = jnp.concatenate([text_ref[...].astype(F32)[EARLY:56], image], 0)
        img[...] = late
        scale = lax.rsqrt(jnp.mean(late * late, -1, keepdims=True) + 1e-06)
        rl[n] = (late * scale * rms_gain_ref[...]).astype(BF16)
        for p in REST:
            send(rl.at[n], rl.at[n], narrow_dev(*p), LATE_IN + index(back(p)))

    def gate_text():
        gate_g.wait_siblings()

        def step(i, carry):
            cols = pl.ds(pl.multiple_of(i * 256, 256), 256)
            gacc[:, cols] = dot(re[...].reshape(8 * EARLY, DU), wg[:, cols])
            return carry
        lax.fori_loop(0, 4, step, 0)

    def up_text():
        up_g.wait_siblings()

        def step(i, carry):
            cols = pl.ds(pl.multiple_of(i * 256, 256), 256)
            up = dot(re[...].reshape(8 * EARLY, DU), wu[:, cols])
            gate = gacc[:, cols]
            inner[:, cols] = (gate / (1.0 + jnp.exp(-gate)) * up).astype(BF16)
            return carry
        lax.fori_loop(0, 4, step, 0)

    def late_inner():
        for p in REST:
            wait(rl.at[near(*p)], LATE_IN + index(p))

        def step(i, carry):
            cols = pl.ds(pl.multiple_of(i * 256, 256), 256)
            rows = rl[...].reshape(8 * LATE, DU)
            gate = dot(rows, wg[:, cols])
            up = dot(rows, wu[:, cols])
            inner_l[:, cols] = (gate / (1.0 + jnp.exp(-gate)) * up).astype(BF16)
            return carry
        lax.fori_loop(0, 4, step, 0)

    def chunk_cols(k):
        return pl.ds(pl.multiple_of(chip(*ORDER[k]) * 512, 512), 512)

    def out_chunk(k):
        place = ORDER[k]
        if k == 0:
            out_g.wait_local()
        out_g.wait_sibling(place)

        def step(i, carry):
            who = chip(*place) * 2 + i
            block = wo[pl.ds(pl.multiple_of(who * 1024, 1024), 1024)]
            cols = pl.ds(pl.multiple_of(who * 256, 256), 256)
            oe[:, :, :, cols] = dot(inner[...], block).astype(BF16).reshape(2, 4, EARLY, 256)
            return carry
        lax.fori_loop(0, 2, step, 0)
        cols = chunk_cols(k)
        for dx in (1, 3, 2):
            to = lax.rem(x + dx, 4)
            send(oe.at[:, to, :, cols], rx.at[3 - dx, :, :, cols], narrow_dev(0, dx), RX + 3 * k + 3 - dx)

    def sum_x(k):
        cols = chunk_cols(k)
        total = oe[1 - yh, x, :, cols].astype(F32)
        for s in range(3):
            wait(rx.at[s, :, :, cols], RX + 3 * k + s)
            total = total + rx[s, 1 - yh, :, cols].astype(F32)
        ys[:, cols] = total.astype(BF16)
        send(ys.at[:, cols], yr.at[:, cols], narrow_dev(1, 0), RY + k)

    def finish(k):
        cols = chunk_cols(k)
        wait(yr.at[:, cols], RY + k)
        total = oe[yh, x, :, cols].astype(F32) + yr[:, cols].astype(F32)
        for s in range(3):
            total = total + rx[s, yh, :, cols].astype(F32)
        res_ref[0:EARLY, cols] = (text_ref[:, cols].astype(F32)[0:EARLY] + total).astype(BF16)

    def late_out():
        def step(i, carry):
            block = wo[pl.ds(pl.multiple_of(i * 1024, 1024), 1024)]
            cols = pl.ds(pl.multiple_of(i * 256, 256), 256)
            ol[:, :, cols] = dot(inner_l[...], block).astype(BF16).reshape(8, LATE, 256)
            return carry
        lax.fori_loop(0, 16, step, 0)
        for p in REST:
            send(ol.at[near(*p)], ro.at[n], narrow_dev(*p), LATE_OUT + index(back(p)))

    def late_finish():
        total = ol[n].astype(F32)
        for p in REST:
            wait(ro.at[near(*p)], LATE_OUT + index(p))
            total = total + ro[near(*p)].astype(F32)
        res_ref[EARLY:64] = (img[...] + total).astype(BF16)

    def events(g, *which):
        for e in which:
            g.event(e)

    stats()
    text_rows()
    text_g.begin()
    layer_norm()
    gate_g.begin()
    for h in (0, 1):
        x_arrivals(h)
        fc1(h)
    events(text_g, 1, 2, 3)
    events(gate_g, 1, 2, 3)
    proj_g.begin()
    gelu(0)
    gelu(1)
    events(text_g, 4, 5, 6, 7)
    events(gate_g, 4, 5, 6, 7)
    up_g.begin()
    fc2(0)
    fc2(1)
    combine(0)
    combine(1)
    events(proj_g, 1, 2, 3)
    gate_text()
    events(proj_g, 4, 5, 6, 7)
    vit_out()
    out_g.begin()
    proj()
    events(up_g, 1, 2, 3)
    image_rows()
    events(up_g, 4, 5, 6, 7)
    up_text()
    events(out_g, 1, 2, 3)
    late_inner()
    for k in range(4):
        out_chunk(k)
    for e, k in ((4, 4), (5, 5), (6, 6)):
        sum_x(k - 4)
        out_g.event(e)
        out_chunk(k)
    sum_x(3)
    out_g.event(7)
    out_chunk(7)
    late_out()
    for k in range(4, 8):
        sum_x(k)
    for k in range(8):
        finish(k)
    late_finish()
    for copy in sends:
        copy.wait_send()


def on_device(vit, ln_gain, w_fc1, b_fc1, w_fc2, b_fc2, w_proj, b_proj, text, rms_gain, w_gate, w_up, w_out):
    vmem = pl.BlockSpec(memory_space=pltpu.VMEM)
    hbm = pl.BlockSpec(memory_space=pl.ANY)
    bf = lambda *shape: pltpu.VMEM(shape, BF16)
    f32 = lambda *shape: pltpu.VMEM(shape, F32)
    dma = pltpu.SemaphoreType.DMA
    vit_out, result = pl.pallas_call(
        kernel,
        out_shape=(jax.ShapeDtypeStruct((64, 768), BF16), jax.ShapeDtypeStruct((64, DU), BF16)),
        in_specs=[vmem] * 6 + [hbm] + [vmem] * 3 + [hbm] * 3,
        out_specs=(vmem, vmem),
        scratch_shapes=[
            bf(4096, 1024), bf(4096, 1024), bf(16 * 1024, 256), bf(16 * 768, 256),
            f32(8, 8, 128), bf(16, 64, 768), bf(8, 8, 16, 768), bf(8, 8, 16, 768), bf(8, 8, 16, 768),
            bf(4, 8, 16, 768), bf(8, 4, 16, 768), bf(8, 16, 2048), bf(8, 16, 2048),
            bf(8, EARLY, DU), bf(8, LATE, DU), f32(8 * EARLY, 1024), bf(8 * EARLY, 1024), bf(8 * LATE, 1024),
            bf(2, 4, EARLY, DU), bf(3, 2, EARLY, DU), bf(EARLY, DU), bf(EARLY, DU),
            bf(8, LATE, DU), bf(8, LATE, DU), f32(LATE, DU),
            dma((4, 24)), dma((4, 20)), dma((12,)), dma((12,)), dma((4,)), dma((128,)), dma((112,)),
        ],
        compiler_params=pltpu.CompilerParams(
            collective_id=0, has_side_effects=True, vmem_limit_bytes=63 * 2**20
        ),
        cost_estimate=pl.CostEstimate(flops=15_300_000_000, bytes_accessed=12_000_000, transcendentals=1_000_000),
    )(
        vit, ln_gain.reshape(1, -1), w_fc1, b_fc1.reshape(1, -1), w_fc2, b_fc2.reshape(1, -1), w_proj,
        b_proj.reshape(1, -1), text, rms_gain.reshape(1, -1), w_gate, w_up, w_out,
    )
    return vit_out, result[56:64], result[0:56]


def solution(mesh):
    return jax.shard_map(
        on_device,
        mesh=mesh,
        in_specs=(
            P("wide", "narrow"),
            P("narrow"),
            P("narrow", "wide"),
            P("wide"),
            P("wide", "narrow"),
            P("narrow"),
            P("narrow", "wide"),
            P(),
            P(("wide", "narrow"), None),
            P(),
            P("wide", "narrow"),
            P("wide", "narrow"),
            P("narrow", "wide"),
        ),
        out_specs=(P("wide", "narrow"), P(("wide", "narrow"), None), P(("wide", "narrow"), None)),
        check_vma=False,
    )
```

time: 745 us -> 243 us (0.33)
  waiting for transfers between devices: 657 us -> 0 us
  Pallas kernels: 0 us -> 234 us
  matrix products: 40.5 us -> 0 us
  blocking collectives: 21.4 us -> 0 us
  between operations: 14 us -> 0.64 us
  other arithmetic: 9.42 us -> 0 us
    all_gather x7 -> x0, waiting for transfers between devices: 373 us -> none  [the longest x1 74 us: on_device(): group_rows = lax.all_gather(rms_rows, 'narrow', axis=0, tiled=True)]
    reduce_scatter x4 -> x0, waiting for transfers between devices: 281 us -> none  [the longest x1 82.9 us: on_device(): lax.psum_scatter(partial_out.astype(jnp.bfloat16), 'narrow', scatter_dime...]
    pallas_call x0 -> x1, Pallas kernels: none -> 234 us  [on_device(): pl.pallas_call(kernel, out_shape=(jax.ShapeDtypeStruct((64, 768), BF16),...]
    dot_general x5 -> x0, matrix products: 40.5 us -> none  [the longest x1 17.3 us: on_device(): jnp.dot(inner, lax.all_gather(w_out, 'wide', axis=1, tiled=True), preferr...]
    psum x1 -> x0, blocking collectives: 21.4 us -> none  [on_device(): lax.psum((jnp.sum(tokens, -1), jnp.sum(tokens * tokens, -1)), 'narrow')]
    convert_element_type x6 -> x0, other arithmetic: 8.09 us -> none  [the longest x1 2.47 us: on_device(): jax.nn.gelu(fc1_sum + b_fc1, approximate=False).astype(jnp.bfloat16)]
  transfers between devices with their start and end apart: 11 -> 0, of which waited for: 11 -> 0; matrix products, arithmetic and copies ran while one was open for 2% -> 0% of each run, Pallas kernels for 0% -> 0%
where the time goes in v1:
time: 243 us
  Pallas kernels  234 us (96%)
  local copies, waits for them, and re-layouts  8.63 us (4%)
    pallas_call x1, Pallas kernels, on_device(): pl.pallas_call(kernel, out_shape=(jax.ShapeDtypeStruct((64, 768), BF16),...  234 us

profile of v1, /device:TPU:1, one launch (start us, length us, event | category | flops | bytes accessed | tf_op | source)
XLA Modules:
  0.0 242.9 jit_solution(7861622392053816830)
XLA Ops:
  0.6 1.3 reshape.21.ln_gain_ref
  1.9 1.3 reshape.22.b1_ref
  3.2 1.3 reshape.23.b2_ref
  4.4 233.7 %shard_map.148 = (bf16[64,768]{1,0:T(8,128)(2,1)}, bf16[64,4096]{1,0:T(8,128)(2,1)}) custom-call(bf16[64,768]{1,0:T(8,128)(2,1)} %vit_ref.1, f32[1,768]{1,0:T(1,128)} %reshape.21.ln_gain_ref, bf16[768,768]{1,0:T(8,128)(2,1)} %wfc1_ref.1, f32[1,768]{1,0:T(1,128)} %reshape.22.b1_ref, bf16[768,768]{1,0:T(8,128)(2,1)} %wfc2_ref.1, f32[1,768]{1,0:T(1,128)} %reshape.23.b2_ref, ...), custom_call_target="tpu_custom_call" | custom-call | flops 15299999744 | bytes 12000000 | tf_op jit(solution)/shard_map/pallas_call | solution.py:486
  238.1 1.5 slice.6
  239.6 1.8 slice.7
  241.4 1.5 copy.17

commit v2 on v1

--- a/solution.py
+++ b/solution.py
@@ -115,14 +115,27 @@
 
 
 def kernel(
-    vit_ref, ln_gain_ref, wfc1_ref, b1_ref, wfc2_ref, b2_ref, wproj_ref, bproj_ref,
-    text_ref, rms_gain_ref, wgate_ref, wup_ref, wout_ref,
+    vit_hbm, ln_gain_ref, wfc1_hbm, b1_ref, wfc2_hbm, b2_ref, wproj_ref, bproj_ref,
+    text_hbm, rms_gain_ref, wgate_ref, wup_ref, wout_ref,
     vout_ref, res_ref,
+    vit_ref, text_ref, wfc1_ref, wfc2_ref,
     wg, wu, wo, wp,
-    stat, xg, part, rs1, hg, sib2, rs2, pp, rp,
+    stat, xg, part, rs1, hg, sib2, rs2, vg, pp, rp, pa, qa,
     re, rl, gacc, inner, inner_l, oe, rx, ys, yr, ol, ro, img,
     wss, wrs, tss, trs, lsem, dss, drs,
 ):
+    loads = [
+        pltpu.make_async_copy(src, dst, lsem.at[4 + k])
+        for k, (src, dst) in enumerate(
+            ((vit_hbm, vit_ref), (text_hbm, text_ref), (wfc1_hbm, wfc1_ref), (wfc2_hbm, wfc2_ref))
+        )
+    ]
+    for load in loads:
+        load.start()
+
+    def row(ref):
+        return ref[...].reshape(1, -1)
+
     w, n = lax.axis_index("wide"), lax.axis_index("narrow")
     c, z, yl = lax.rem(w, 2), lax.rem(w // 2, 4), w // 8
     x, yh = lax.rem(n, 4), n // 4
@@ -173,7 +186,9 @@
             device_id=sib, device_id_type=MESH,
         ).wait_recv()
 
-    STAT, X, XSIB, RS1, HID, COMB, RS2, PROJ, LATE_IN, LATE_OUT, RX, RY = 0, 7, 14, 22, 36, 50, 52, 59, 66, 73, 80, 104
+    STAT, X, XSIB, RS1, HID, COMB, RS2, PROJ, LATE_IN, LATE_OUT, RX, RY, VG, PA, WP = (
+        0, 7, 14, 22, 36, 50, 52, 59, 66, 73, 80, 104, 112, 115, 118
+    )
 
     def rows_of(buf, rows):
         def slot(dy, dz, other):
@@ -190,7 +205,6 @@
     gate_g = gather(0, wgate_ref, wg, 256)
     up_g = gather(1, wup_ref, wu, 256)
     out_g = gather(2, wout_ref, wo, 1024)
-    proj_g = gather(3, wproj_ref, wp, 768)
 
     def text_slot(dy, dx, other):
         return re.at[near(dy, dx)]
@@ -201,6 +215,7 @@
     )
 
     def stats():
+        loads[0].wait()
         rows = vit_ref[...].astype(F32)
         total = jnp.sum(rows, -1, keepdims=True)
         square = jnp.sum(rows * rows, -1, keepdims=True)
@@ -212,9 +227,10 @@
             send(stat.at[n], stat.at[n], narrow_dev(*p), STAT + index(back(p)))
 
     def text_rows():
+        loads[1].wait()
         rows = text_ref[...].astype(F32)
         scale = lax.rsqrt(jnp.mean(rows * rows, -1, keepdims=True) + 1e-06)
-        normed = rows * scale * rms_gain_ref[...]
+        normed = rows * scale * row(rms_gain_ref)
         re[n] = normed[0:EARLY].astype(BF16)
 
     def layer_norm():
@@ -228,7 +244,7 @@
         variance = turned[0:64, 1:2] / DV - mean * mean
         scale = lax.rsqrt(variance + 1e-06)
         rows = vit_ref[...].astype(F32)
-        xg[w] = ((rows - mean) * scale * ln_gain_ref[...]).astype(BF16)
+        xg[w] = ((rows - mean) * scale * row(ln_gain_ref)).astype(BF16)
         for p in REST:
             send(xg.at[w], xg.at[w], wide_dev(*p), X + index(back(p)))
         send(xg.at[w], xg.at[w], sib, XSIB)
@@ -249,6 +265,9 @@
     rs1_sends = {0: [], 1: []}
 
     def fc1(h):
+        if h == 0:
+            loads[2].wait()
+
         def step(i, carry):
             first = half_start(h) + 2 * i
             rows = xg[pl.ds(first * 2, 4)].reshape(256, 768)
@@ -269,13 +288,15 @@
         for p in REST:
             wait(rs1.at[near(*p), chips], RS1 + 7 * h + index(p))
             total = total + rs1[near(*p), chips].astype(F32)
-        v = total.reshape(64, 768) + b1_ref[...]
+        v = total.reshape(64, 768) + row(b1_ref)
         hidden = 0.5 * v * (1.0 + lax.erf(v * (0.5 ** 0.5)))
         hg[n, chips] = hidden.astype(BF16).reshape(4, 16, 768)
         for p in REST:
             send(hg.at[n, chips], hg.at[n, chips], narrow_dev(*p), HID + 7 * h + index(back(p)))
 
     def fc2(h):
+        if h == 0:
+            loads[3].wait()
         chips = pl.ds(half_start(h), 4)
         for p in REST:
             wait(hg.at[near(*p), chips], HID + 7 * h + index(p))
@@ -304,33 +325,65 @@
         for p in REST:
             wait(rs2.at[chip(*p)], RS2 + index(p))
             total = total + rs2[chip(*p)].astype(F32)
-        rows = vit_ref[...].astype(F32) + total.reshape(64, 768) + b2_ref[...]
-        vout_ref[...] = rows.astype(BF16)
+        rows = vit_ref[...].astype(F32) + total.reshape(64, 768) + row(b2_ref)
+        image = rows.astype(BF16)
+        vout_ref[...] = image
+        vg[z] = image
+        for dz in (1, 3, 2):
+            send(vg.at[z], vg.at[z], wide_dev(0, dz), VG + 3 - dz)
+
+    def weights_at(dy, core):
+        start = (lax.rem(yl + dy, 2) * 2 + core) * 768
+        return wp.at[pl.ds(pl.multiple_of(start, 768), 768)]
+
+    proj_local = pltpu.make_async_copy(wproj_ref, weights_at(0, c), lsem.at[3])
+
+    def proj_begin():
+        mine = weights_at(0, c)
+        send(wproj_ref, mine, wide_dev(1, 0), WP)
+        send(wproj_ref, mine, sib, WP + 1)
+        proj_local.start()
+
+    def proj_share():
+        ref = weights_at(1, c)
+        wait(ref, WP)
+        send(ref, ref, sib, WP + 2)
 
     def proj():
-        proj_g.wait_siblings()
-
-        def step(i, carry):
-            rows = vout_ref[...]
-            low = dot(rows, wp[pl.ds(pl.multiple_of(i * 768, 768), 768)]).reshape(8, 8, 256)
-            high = dot(rows, wp[pl.ds(pl.multiple_of((i + 8) * 768, 768), 768)]).reshape(8, 8, 256)
-            pp[:, :, pl.ds(pl.multiple_of(i * 256, 256), 256)] = jnp.concatenate([low, high], 1).astype(BF16)
-            return carry
-        lax.fori_loop(0, 8, step, 0)
+        proj_local.wait()
+        wait(weights_at(0, 1 - c), WP + 1)
+        wait(weights_at(1, 1 - c), WP + 2)
+        for dz in (1, 3, 2):
+            wait(vg.at[lax.rem(z + dz, 4)], VG + dz - 1)
+        for i in range(2):
+            rows = vg[...].reshape(256, 768)
+            low = dot(rows, wp[i * 768:(i + 1) * 768]).reshape(4, 8, 8, 256)
+            high = dot(rows, wp[(i + 2) * 768:(i + 3) * 768]).reshape(4, 8, 8, 256)
+            for k in range(4):
+                pp[:, k, :, i * 256:(i + 1) * 256] = jnp.concatenate([low[k], high[k]], 1).astype(BF16)
         for p in REST:
             send(pp.at[near(*p)], rp.at[n], narrow_dev(*p), PROJ + index(back(p)))
 
-    def image_rows():
+    def proj_sum():
         total = pp[n].astype(F32)
         for p in REST:
             wait(rp.at[near(*p)], PROJ + index(p))
             total = total + rp[near(*p)].astype(F32)
-        rows = jnp.concatenate([total[0:8], total[8:16]], 1) + bproj_ref[...]
+        pa[...] = total
+        qa[z] = pa[z]
+        for dz in (1, 3, 2):
+            send(pa.at[lax.rem(z + dz, 4)], qa.at[z], wide_dev(0, dz), PA + 3 - dz)
+
+    def image_rows():
+        for dz in (1, 3, 2):
+            wait(qa.at[lax.rem(z + dz, 4)], PA + dz - 1)
+        sums = [qa[k, 0:8] for k in range(4)] + [qa[k, 8:16] for k in range(4)]
+        rows = jnp.concatenate(sums, 1) + row(bproj_ref)
         image = rows.astype(BF16).astype(F32)
         late = jnp.concatenate([text_ref[...].astype(F32)[EARLY:56], image], 0)
         img[...] = late
         scale = lax.rsqrt(jnp.mean(late * late, -1, keepdims=True) + 1e-06)
-        rl[n] = (late * scale * rms_gain_ref[...]).astype(BF16)
+        rl[n] = (late * scale * row(rms_gain_ref)).astype(BF16)
         for p in REST:
             send(rl.at[n], rl.at[n], narrow_dev(*p), LATE_IN + index(back(p)))
 
@@ -428,53 +481,93 @@
 
     stats()
     text_rows()
+    gate_g.begin()
     text_g.begin()
+    gate_g.event(1)
+    gate_g.event(2)
+    up_g.begin()
+    text_g.event(3)
     layer_norm()
-    gate_g.begin()
-    for h in (0, 1):
-        x_arrivals(h)
-        fc1(h)
-    events(text_g, 1, 2, 3)
-    events(gate_g, 1, 2, 3)
-    proj_g.begin()
+    gate_g.event(3)
+    x_arrivals(0)
+    fc1(0)
+    x_arrivals(1)
+    up_g.event(2)
+    fc1(1)
+    up_g.event(3)
     gelu(0)
+    gate_g.event(5)
     gelu(1)
-    events(text_g, 4, 5, 6, 7)
-    events(gate_g, 4, 5, 6, 7)
-    up_g.begin()
+    text_g.event(1)
+    up_g.event(1)
+    gate_g.event(4)
+    gate_g.event(6)
+    text_g.event(6)
+    up_g.event(5)
+    out_g.begin()
     fc2(0)
+    up_g.event(6)
+    gate_g.event(7)
+    text_g.event(2)
+    text_g.event(5)
     fc2(1)
+    text_g.event(4)
+    combine(1)
     combine(0)
-    combine(1)
-    events(proj_g, 1, 2, 3)
+    proj_begin()
+    up_g.event(7)
+    text_g.event(7)
+    up_g.event(4)
     gate_text()
-    events(proj_g, 4, 5, 6, 7)
+    up_text()
     vit_out()
-    out_g.begin()
+    out_chunk(0)
+    out_g.event(1)
+    out_g.event(2)
+    out_chunk(2)
+    proj_share()
     proj()
-    events(up_g, 1, 2, 3)
+    out_g.event(4)
+    out_g.event(3)
+    out_chunk(4)
+    proj_sum()
+    out_chunk(3)
     image_rows()
-    events(up_g, 4, 5, 6, 7)
-    up_text()
-    events(out_g, 1, 2, 3)
+    out_g.event(5)
+    out_g.event(6)
+    out_g.event(7)
+    out_chunk(5)
+    out_chunk(6)
+    sum_x(0)
+    sum_x(3)
+    out_chunk(7)
     late_inner()
-    for k in range(4):
-        out_chunk(k)
-    for e, k in ((4, 4), (5, 5), (6, 6)):
-        sum_x(k - 4)
-        out_g.event(e)
-        out_chunk(k)
-    sum_x(3)
-    out_g.event(7)
-    out_chunk(7)
+    out_chunk(1)
+    sum_x(4)
+    sum_x(2)
     late_out()
-    for k in range(4, 8):
-        sum_x(k)
-    for k in range(8):
-        finish(k)
+    sum_x(5)
+    finish(3)
+    sum_x(6)
+    sum_x(7)
+    sum_x(1)
+    finish(7)
+    finish(6)
+    finish(4)
+    finish(0)
+    finish(2)
+    finish(5)
     late_finish()
+    finish(1)
     for copy in sends:
         copy.wait_send()
+
+
+def split(vit_ref, rows_ref, vit_out_ref, image_ref, text_ref):
+    vit_out_ref[...] = vit_ref[...]
+    rows = rows_ref[...].astype(F32)
+    image_ref[...] = rows[56:64].astype(BF16)
+    text_ref[...] = rows[0:56].astype(BF16)
 
 
 def on_device(vit, ln_gain, w_fc1, b_fc1, w_fc2, b_fc2, w_proj, b_proj, text, rms_gain, w_gate, w_up, w_out):
@@ -483,29 +576,37 @@
     bf = lambda *shape: pltpu.VMEM(shape, BF16)
     f32 = lambda *shape: pltpu.VMEM(shape, F32)
     dma = pltpu.SemaphoreType.DMA
-    vit_out, result = pl.pallas_call(
+    vit_rows, result = pl.pallas_call(
         kernel,
         out_shape=(jax.ShapeDtypeStruct((64, 768), BF16), jax.ShapeDtypeStruct((64, DU), BF16)),
-        in_specs=[vmem] * 6 + [hbm] + [vmem] * 3 + [hbm] * 3,
+        in_specs=[hbm, vmem, hbm, vmem, hbm, vmem, hbm, vmem, hbm, vmem, hbm, hbm, hbm],
         out_specs=(vmem, vmem),
         scratch_shapes=[
-            bf(4096, 1024), bf(4096, 1024), bf(16 * 1024, 256), bf(16 * 768, 256),
+            bf(64, 768), bf(56, DU), bf(768, 768), bf(768, 768),
+            bf(4096, 1024), bf(4096, 1024), bf(16 * 1024, 256), bf(4 * 768, 256),
             f32(8, 8, 128), bf(16, 64, 768), bf(8, 8, 16, 768), bf(8, 8, 16, 768), bf(8, 8, 16, 768),
-            bf(4, 8, 16, 768), bf(8, 4, 16, 768), bf(8, 16, 2048), bf(8, 16, 2048),
+            bf(4, 8, 16, 768), bf(8, 4, 16, 768), bf(4, 64, 768),
+            bf(8, 4, 16, 512), bf(8, 4, 16, 512), f32(4, 16, 512), f32(4, 16, 512),
             bf(8, EARLY, DU), bf(8, LATE, DU), f32(8 * EARLY, 1024), bf(8 * EARLY, 1024), bf(8 * LATE, 1024),
             bf(2, 4, EARLY, DU), bf(3, 2, EARLY, DU), bf(EARLY, DU), bf(EARLY, DU),
             bf(8, LATE, DU), bf(8, LATE, DU), f32(LATE, DU),
-            dma((4, 24)), dma((4, 20)), dma((12,)), dma((12,)), dma((4,)), dma((128,)), dma((112,)),
+            dma((3, 24)), dma((3, 20)), dma((12,)), dma((12,)), dma((8,)), dma((128,)), dma((124,)),
         ],
         compiler_params=pltpu.CompilerParams(
             collective_id=0, has_side_effects=True, vmem_limit_bytes=63 * 2**20
         ),
         cost_estimate=pl.CostEstimate(flops=15_300_000_000, bytes_accessed=12_000_000, transcendentals=1_000_000),
-    )(
-        vit, ln_gain.reshape(1, -1), w_fc1, b_fc1.reshape(1, -1), w_fc2, b_fc2.reshape(1, -1), w_proj,
-        b_proj.reshape(1, -1), text, rms_gain.reshape(1, -1), w_gate, w_up, w_out,
-    )
-    return vit_out, result[56:64], result[0:56]
+    )(vit, ln_gain, w_fc1, b_fc1, w_fc2, b_fc2, w_proj, b_proj, text, rms_gain, w_gate, w_up, w_out)
+    return pl.pallas_call(
+        split,
+        out_shape=(
+            jax.ShapeDtypeStruct((64, 768), BF16),
+            jax.ShapeDtypeStruct((8, DU), BF16),
+            jax.ShapeDtypeStruct((56, DU), BF16),
+        ),
+        in_specs=[vmem] * 2,
+        out_specs=(vmem, vmem, vmem),
+    )(vit_rows, result)
 
 
 def solution(mesh):

time: 243 us -> 188 us (0.77)
  Pallas kernels: 234 us -> 186 us
  local copies, waits for them, and re-layouts: 8.63 us -> 0 us
    pallas_call x1, Pallas kernels: 234 us -> 184 us  [on_device(): pl.pallas_call(kernel, out_shape=(jax.ShapeDtypeStruct((64, 768), BF16),...]
    reshape x3 -> x0, local copies, waits for them, and re-layouts: 3.8 us -> none  [the longest x1 1.27 us: on_device(): ln_gain.reshape(1, -1)]
    slice x2 -> x0, local copies, waits for them, and re-layouts: 3.29 us -> none  [on_device(): return (vit_out, result[56:64], result[0:56])]
where the time goes in v2:
time: 188 us; the launch traced here: 187 us
  Pallas kernels  186 us (99%)
    pallas_call x1, Pallas kernels, on_device(): pl.pallas_call(kernel, out_shape=(jax.ShapeDtypeStruct((64, 768), BF16),...  184 us

profile of v2, /device:TPU:1, one launch (start us, length us, event | category | flops | bytes accessed | tf_op | source)
XLA Modules:
  0.0 186.5 jit_solution(18037861278248398544)
XLA Ops:
  0.6 184.0 %shard_map.148 = (bf16[64,768]{1,0:T(8,128)(2,1)}, bf16[64,4096]{1,0:T(8,128)(2,1)}) custom-call(bf16[64,768]{1,0:T(8,128)(2,1)} %vit_hbm.1, f32[768]{0:T(1024)} %ln_gain_ref.1, bf16[768,768]{1,0:T(8,128)(2,1)} %wfc1_hbm.1, f32[768]{0:T(1024)} %b1_ref.1, bf16[768,768]{1,0:T(8,128)(2,1)} %wfc2_hbm.1, f32[768]{0:T(1024)} %b2_ref.1, ...), custom_call_target="tpu_custom_call" | custom-call | flops 15299999744 | bytes 12000000 | tf_op jit(solution)/shard_map/pallas_call | solution.py:579
  184.6 1.9 %shard_map.149 = (bf16[64,768]{1,0:T(8,128)(2,1)}, bf16[8,4096]{1,0:T(8,128)(2,1)}, bf16[56,4096]{1,0:T(8,128)(2,1)}) custom-call(bf16[64,768]{1,0:T(8,128)(2,1)} %get-tuple-element.5.vit_ref, bf16[64,4096]{1,0:T(8,128)(2,1)} %get-tuple-element.6.rows_ref), custom_call_target="tpu_custom_call" | custom-call | tf_op jit(solution)/shard_map/pallas_call | solution.py:600

commit v3 on v2

--- a/solution.py
+++ b/solution.py
@@ -12,6 +12,7 @@
 MESH = pl.DeviceIdType.MESH
 EARLY = 48
 LATE = 16
+PAIR_FIRST = (1, 2, 3, 4,)
 REST = [(0, 1), (0, 3), (1, 0), (0, 2), (1, 1), (1, 3), (1, 2)]
 PLACES = [(0, 0)] + REST
 ORDER = [(0, 0), (0, 3), (0, 1), (1, 0), (0, 2), (1, 3), (1, 1), (1, 2)]
@@ -121,7 +122,7 @@
     vit_ref, text_ref, wfc1_ref, wfc2_ref,
     wg, wu, wo, wp,
     stat, xg, part, rs1, hg, sib2, rs2, vg, pp, rp, pa, qa,
-    re, rl, gacc, inner, inner_l, oe, rx, ys, yr, ol, ro, img,
+    re, rl, gacc, inner, inner_l, oe, rx, ryb, ys, yr, ol, ro, img,
     wss, wrs, tss, trs, lsem, dss, drs,
 ):
     loads = [
@@ -186,8 +187,8 @@
             device_id=sib, device_id_type=MESH,
         ).wait_recv()
 
-    STAT, X, XSIB, RS1, HID, COMB, RS2, PROJ, LATE_IN, LATE_OUT, RX, RY, VG, PA, WP = (
-        0, 7, 14, 22, 36, 50, 52, 59, 66, 73, 80, 104, 112, 115, 118
+    STAT, X, XSIB, RS1, HID, COMB, RS2, PROJ, LATE_IN, LATE_OUT, RX, RY, VG, PA, WP, RXB = (
+        0, 7, 14, 22, 36, 50, 52, 59, 66, 73, 80, 104, 112, 115, 118, 124
     )
 
     def rows_of(buf, rows):
@@ -277,28 +278,50 @@
             return carry
         lax.fori_loop(0, 2, step, 0)
         chips = pl.ds(half_start(h), 4)
-        for p in REST:
-            rs1_sends[h].append(
-                send(part.at[near(*p), chips], rs1.at[n, chips], narrow_dev(*p), RS1 + 7 * h + index(back(p)), False)
-            )
+        for dy in (1, 0):
+            for dx in (1, 3, 2):
+                rs1_sends[h].append(
+                    send(
+                        part.at[near(dy, dx), chips], rs1.at[near(dy, 0), chips], narrow_dev(0, dx),
+                        RS1 + 7 * h + index((dy, 4 - dx)), False,
+                    )
+                )
+
+    def pair_sum(h):
+        chips = pl.ds(half_start(h), 4)
+        total = part[near(1, 0), chips].astype(F32)
+        for dx in (1, 3, 2):
+            wait(rs1.at[near(1, dx), chips], RS1 + 7 * h + index((1, dx)))
+            total = total + rs1[near(1, dx), chips].astype(F32)
+        part[near(1, 0), chips] = total.astype(BF16)
+        rs1_sends[h].append(
+            send(part.at[near(1, 0), chips], rs1.at[n, chips], narrow_dev(1, 0), RS1 + 7 * h + index((1, 0)), False)
+        )
 
     def gelu(h):
         chips = pl.ds(half_start(h), 4)
         total = part[n, chips].astype(F32)
-        for p in REST:
+        for p in ((0, 1), (0, 3), (0, 2), (1, 0)):
             wait(rs1.at[near(*p), chips], RS1 + 7 * h + index(p))
             total = total + rs1[near(*p), chips].astype(F32)
         v = total.reshape(64, 768) + row(b1_ref)
         hidden = 0.5 * v * (1.0 + lax.erf(v * (0.5 ** 0.5)))
         hg[n, chips] = hidden.astype(BF16).reshape(4, 16, 768)
-        for p in REST:
+        for p in ((1, 0), (0, 1), (0, 3), (0, 2)):
             send(hg.at[n, chips], hg.at[n, chips], narrow_dev(*p), HID + 7 * h + index(back(p)))
+
+    def pass_hidden(h):
+        chips = pl.ds(half_start(h), 4)
+        ref = hg.at[near(1, 0), chips]
+        wait(ref, HID + 7 * h + index((1, 0)))
+        for dx in (1, 3, 2):
+            send(ref, ref, narrow_dev(0, dx), HID + 7 * h + index((1, 4 - dx)))
 
     def fc2(h):
         if h == 0:
             loads[3].wait()
         chips = pl.ds(half_start(h), 4)
-        for p in REST:
+        for p in [q for q in REST if q != (1, 0)]:
             wait(hg.at[near(*p), chips], HID + 7 * h + index(p))
         for copy in rs1_sends[h]:
             copy.wait_send()
@@ -384,8 +407,14 @@
         img[...] = late
         scale = lax.rsqrt(jnp.mean(late * late, -1, keepdims=True) + 1e-06)
         rl[n] = (late * scale * row(rms_gain_ref)).astype(BF16)
-        for p in REST:
+        for p in ((1, 0), (0, 1), (0, 3), (0, 2)):
             send(rl.at[n], rl.at[n], narrow_dev(*p), LATE_IN + index(back(p)))
+
+    def pass_late():
+        ref = rl.at[near(1, 0)]
+        wait(ref, LATE_IN + index((1, 0)))
+        for dx in (1, 3, 2):
+            send(ref, ref, narrow_dev(0, dx), LATE_IN + index((1, 4 - dx)))
 
     def gate_text():
         gate_g.wait_siblings()
@@ -408,7 +437,7 @@
         lax.fori_loop(0, 4, step, 0)
 
     def late_inner():
-        for p in REST:
+        for p in [q for q in REST if q != (1, 0)]:
             wait(rl.at[near(*p)], LATE_IN + index(p))
 
         def step(i, carry):
@@ -437,12 +466,23 @@
             return carry
         lax.fori_loop(0, 2, step, 0)
         cols = chunk_cols(k)
+        if k in PAIR_FIRST:
+            send(oe.at[1 - yh, :, :, cols], ryb.at[:, :, cols], narrow_dev(1, 0), RX + 3 * k)
+            return
         for dx in (1, 3, 2):
             to = lax.rem(x + dx, 4)
             send(oe.at[:, to, :, cols], rx.at[3 - dx, :, :, cols], narrow_dev(0, dx), RX + 3 * k + 3 - dx)
 
     def sum_x(k):
         cols = chunk_cols(k)
+        if k in PAIR_FIRST:
+            wait(ryb.at[:, :, cols], RX + 3 * k)
+            total = oe[yh, :, :, cols].astype(F32) + ryb[:, :, cols].astype(F32)
+            oe[yh, :, :, cols] = total.astype(BF16)
+            for dx in (1, 3, 2):
+                to = lax.rem(x + dx, 4)
+                send(oe.at[yh, to, :, cols], rx.at[3 - dx, 0, :, cols], narrow_dev(0, dx), RXB + 3 * k + 3 - dx)
+            return
         total = oe[1 - yh, x, :, cols].astype(F32)
         for s in range(3):
             wait(rx.at[s, :, :, cols], RX + 3 * k + s)
@@ -452,10 +492,16 @@
 
     def finish(k):
         cols = chunk_cols(k)
-        wait(yr.at[:, cols], RY + k)
-        total = oe[yh, x, :, cols].astype(F32) + yr[:, cols].astype(F32)
-        for s in range(3):
-            total = total + rx[s, yh, :, cols].astype(F32)
+        total = oe[yh, x, :, cols].astype(F32)
+        if k in PAIR_FIRST:
+            for s in range(3):
+                wait(rx.at[s, 0, :, cols], RXB + 3 * k + s)
+                total = total + rx[s, 0, :, cols].astype(F32)
+        else:
+            wait(yr.at[:, cols], RY + k)
+            total = total + yr[:, cols].astype(F32)
+            for s in range(3):
+                total = total + rx[s, yh, :, cols].astype(F32)
         res_ref[0:EARLY, cols] = (text_ref[:, cols].astype(F32)[0:EARLY] + total).astype(BF16)
 
     def late_out():
@@ -480,85 +526,90 @@
             g.event(e)
 
     stats()
-    text_rows()
     gate_g.begin()
-    text_g.begin()
-    gate_g.event(1)
-    gate_g.event(2)
+    layer_norm()
     up_g.begin()
-    text_g.event(3)
-    layer_norm()
     gate_g.event(3)
     x_arrivals(0)
     fc1(0)
     x_arrivals(1)
+    fc1(1)
+    pair_sum(0)
+    pair_sum(1)
+    up_g.event(3)
     up_g.event(2)
-    fc1(1)
-    up_g.event(3)
     gelu(0)
+    gate_g.event(2)
+    gelu(1)
+    gate_g.event(1)
+    text_rows()
+    pass_hidden(0)
+    pass_hidden(1)
+    text_g.begin()
+    proj_begin()
+    fc2(0)
+    combine(0)
+    fc2(1)
+    combine(1)
+    up_g.event(1)
+    gate_g.event(6)
+    text_g.event(3)
+    text_g.event(2)
+    gate_g.event(4)
     gate_g.event(5)
-    gelu(1)
     text_g.event(1)
-    up_g.event(1)
-    gate_g.event(4)
-    gate_g.event(6)
+    vit_out()
+    text_g.event(4)
+    proj_share()
+    up_g.event(6)
+    up_g.event(5)
+    up_g.event(4)
+    out_g.begin()
+    text_g.event(5)
     text_g.event(6)
-    up_g.event(5)
-    out_g.begin()
-    fc2(0)
-    up_g.event(6)
+    text_g.event(7)
+    proj()
     gate_g.event(7)
-    text_g.event(2)
-    text_g.event(5)
-    fc2(1)
-    text_g.event(4)
-    combine(1)
-    combine(0)
-    proj_begin()
+    gate_text()
     up_g.event(7)
-    text_g.event(7)
-    up_g.event(4)
-    gate_text()
     up_text()
-    vit_out()
     out_chunk(0)
+    proj_sum()
+    out_g.event(3)
     out_g.event(1)
+    image_rows()
     out_g.event(2)
     out_chunk(2)
-    proj_share()
-    proj()
-    out_g.event(4)
-    out_g.event(3)
-    out_chunk(4)
-    proj_sum()
     out_chunk(3)
-    image_rows()
+    pass_late()
+    sum_x(2)
+    out_g.event(6)
     out_g.event(5)
-    out_g.event(6)
-    out_g.event(7)
-    out_chunk(5)
+    out_chunk(1)
     out_chunk(6)
     sum_x(0)
     sum_x(3)
+    out_chunk(5)
+    out_g.event(4)
+    late_inner()
+    finish(2)
+    out_g.event(7)
+    out_chunk(4)
+    sum_x(6)
     out_chunk(7)
-    late_inner()
-    out_chunk(1)
+    late_out()
+    sum_x(1)
+    sum_x(5)
+    sum_x(7)
     sum_x(4)
-    sum_x(2)
-    late_out()
-    sum_x(5)
+    late_finish()
     finish(3)
-    sum_x(6)
-    sum_x(7)
-    sum_x(1)
+    finish(5)
+    finish(0)
+    finish(6)
+    finish(1)
     finish(7)
-    finish(6)
     finish(4)
-    finish(0)
-    finish(2)
-    finish(5)
-    late_finish()
-    finish(1)
     for copy in sends:
         copy.wait_send()
 
@@ -588,9 +639,9 @@
             bf(4, 8, 16, 768), bf(8, 4, 16, 768), bf(4, 64, 768),
             bf(8, 4, 16, 512), bf(8, 4, 16, 512), f32(4, 16, 512), f32(4, 16, 512),
             bf(8, EARLY, DU), bf(8, LATE, DU), f32(8 * EARLY, 1024), bf(8 * EARLY, 1024), bf(8 * LATE, 1024),
-            bf(2, 4, EARLY, DU), bf(3, 2, EARLY, DU), bf(EARLY, DU), bf(EARLY, DU),
+            bf(2, 4, EARLY, DU), bf(3, 2, EARLY, DU), bf(4, EARLY, DU), bf(EARLY, DU), bf(EARLY, DU),
             bf(8, LATE, DU), bf(8, LATE, DU), f32(LATE, DU),
-            dma((3, 24)), dma((3, 20)), dma((12,)), dma((12,)), dma((8,)), dma((128,)), dma((124,)),
+            dma((3, 24)), dma((3, 20)), dma((12,)), dma((12,)), dma((8,)), dma((128,)), dma((148,)),
         ],
         compiler_params=pltpu.CompilerParams(
             collective_id=0, has_side_effects=True, vmem_limit_bytes=63 * 2**20

time: 188 us -> 172 us (0.915)
  Pallas kernels: 186 us -> 171 us
    pallas_call x1, Pallas kernels: 184 us -> 169 us  [on_device(): pl.pallas_call(kernel, out_shape=(jax.ShapeDtypeStruct((64, 768), BF16),...]
where the time goes in v3:
time: 172 us; the launch traced here: 171 us
  Pallas kernels  171 us (99%)
    pallas_call x1, Pallas kernels, on_device(): pl.pallas_call(kernel, out_shape=(jax.ShapeDtypeStruct((64, 768), BF16),...  169 us

profile of v3, /device:TPU:1, one launch (start us, length us, event | category | flops | bytes accessed | tf_op | source)
XLA Modules:
  0.0 171.4 jit_solution(8842105368955778963)
XLA Ops:
  0.6 168.8 %shard_map.148 = (bf16[64,768]{1,0:T(8,128)(2,1)}, bf16[64,4096]{1,0:T(8,128)(2,1)}) custom-call(bf16[64,768]{1,0:T(8,128)(2,1)} %vit_hbm.1, f32[768]{0:T(1024)} %ln_gain_ref.1, bf16[768,768]{1,0:T(8,128)(2,1)} %wfc1_hbm.1, f32[768]{0:T(1024)} %b1_ref.1, bf16[768,768]{1,0:T(8,128)(2,1)} %wfc2_hbm.1, f32[768]{0:T(1024)} %b2_ref.1, ...), custom_call_target="tpu_custom_call" | custom-call | flops 15299999744 | bytes 12000000 | tf_op jit(solution)/shard_map/pallas_call | solution.py:630
  169.5 1.9 %shard_map.149 = (bf16[64,768]{1,0:T(8,128)(2,1)}, bf16[8,4096]{1,0:T(8,128)(2,1)}, bf16[56,4096]{1,0:T(8,128)(2,1)}) custom-call(bf16[64,768]{1,0:T(8,128)(2,1)} %get-tuple-element.5.vit_ref, bf16[64,4096]{1,0:T(8,128)(2,1)} %get-tuple-element.6.rows_ref), custom_call_target="tpu_custom_call" | custom-call | tf_op jit(solution)/shard_map/pallas_call | solution.py:651

commit v4 on v3

--- a/solution.py
+++ b/solution.py
@@ -187,8 +187,8 @@
             device_id=sib, device_id_type=MESH,
         ).wait_recv()
 
-    STAT, X, XSIB, RS1, HID, COMB, RS2, PROJ, LATE_IN, LATE_OUT, RX, RY, VG, PA, WP, RXB = (
-        0, 7, 14, 22, 36, 50, 52, 59, 66, 73, 80, 104, 112, 115, 118, 124
+    STAT, X, XSIB, RS1, HID, COMB, RS2, PROJ, LATE_IN, LATE_OUT, RX, RY, VG, PA, WP, RXB, LATE_OUT2 = (
+        0, 7, 14, 22, 36, 50, 52, 59, 66, 73, 80, 104, 112, 115, 118, 124, 148
     )
 
     def rows_of(buf, rows):
@@ -504,20 +504,27 @@
                 total = total + rx[s, yh, :, cols].astype(F32)
         res_ref[0:EARLY, cols] = (text_ref[:, cols].astype(F32)[0:EARLY] + total).astype(BF16)
 
-    def late_out():
+    def late_half(e):
+        return pl.ds(e * DU // 2, DU // 2)
+
+    def late_out(e):
         def step(i, carry):
             block = wo[pl.ds(pl.multiple_of(i * 1024, 1024), 1024)]
             cols = pl.ds(pl.multiple_of(i * 256, 256), 256)
             ol[:, :, cols] = dot(inner_l[...], block).astype(BF16).reshape(8, LATE, 256)
             return carry
-        lax.fori_loop(0, 16, step, 0)
-        for p in REST:
-            send(ol.at[near(*p)], ro.at[n], narrow_dev(*p), LATE_OUT + index(back(p)))
+        lax.fori_loop(8 * e, 8 * e + 8, step, 0)
+        for p in REST:
+            send(
+                ol.at[near(*p), :, late_half(e)], ro.at[n, :, late_half(e)], narrow_dev(*p),
+                (LATE_OUT, LATE_OUT2)[e] + index(back(p)),
+            )
 
     def late_finish():
         total = ol[n].astype(F32)
         for p in REST:
-            wait(ro.at[near(*p)], LATE_OUT + index(p))
+            for e in range(2):
+                wait(ro.at[near(*p), :, late_half(e)], (LATE_OUT, LATE_OUT2)[e] + index(p))
             total = total + ro[near(*p)].astype(F32)
         res_ref[EARLY:64] = (img[...] + total).astype(BF16)
 
@@ -597,7 +604,8 @@
     out_chunk(4)
     sum_x(6)
     out_chunk(7)
-    late_out()
+    late_out(0)
+    late_out(1)
     sum_x(1)
     sum_x(5)
     sum_x(7)
@@ -641,7 +649,7 @@
             bf(8, EARLY, DU), bf(8, LATE, DU), f32(8 * EARLY, 1024), bf(8 * EARLY, 1024), bf(8 * LATE, 1024),
             bf(2, 4, EARLY, DU), bf(3, 2, EARLY, DU), bf(4, EARLY, DU), bf(EARLY, DU), bf(EARLY, DU),
             bf(8, LATE, DU), bf(8, LATE, DU), f32(LATE, DU),
-            dma((3, 24)), dma((3, 20)), dma((12,)), dma((12,)), dma((8,)), dma((128,)), dma((148,)),
+            dma((3, 24)), dma((3, 20)), dma((12,)), dma((12,)), dma((8,)), dma((136,)), dma((156,)),
         ],
         compiler_params=pltpu.CompilerParams(
             collective_id=0, has_side_effects=True, vmem_limit_bytes=63 * 2**20

time: 172 us -> 171 us (level)
  no operation moved by 1% of the time
where the time goes in v4:
time: 171 us
  Pallas kernels  170 us (99%)
    pallas_call x1, Pallas kernels, on_device(): pl.pallas_call(kernel, out_shape=(jax.ShapeDtypeStruct((64, 768), BF16),...  168 us

profile of v4, /device:TPU:1, one launch (start us, length us, event | category | flops | bytes accessed | tf_op | source)
XLA Modules:
  0.0 170.5 jit_solution(14171004290226595902)
XLA Ops:
  0.6 168.0 %shard_map.148 = (bf16[64,768]{1,0:T(8,128)(2,1)}, bf16[64,4096]{1,0:T(8,128)(2,1)}) custom-call(bf16[64,768]{1,0:T(8,128)(2,1)} %vit_hbm.1, f32[768]{0:T(1024)} %ln_gain_ref.1, bf16[768,768]{1,0:T(8,128)(2,1)} %wfc1_hbm.1, f32[768]{0:T(1024)} %b1_ref.1, bf16[768,768]{1,0:T(8,128)(2,1)} %wfc2_hbm.1, f32[768]{0:T(1024)} %b2_ref.1, ...), custom_call_target="tpu_custom_call" | custom-call | flops 15299999744 | bytes 12000000 | tf_op jit(solution)/shard_map/pallas_call | solution.py:638
  168.6 1.9 %shard_map.149 = (bf16[64,768]{1,0:T(8,128)(2,1)}, bf16[8,4096]{1,0:T(8,128)(2,1)}, bf16[56,4096]{1,0:T(8,128)(2,1)}) custom-call(bf16[64,768]{1,0:T(8,128)(2,1)} %get-tuple-element.5.vit_ref, bf16[64,4096]{1,0:T(8,128)(2,1)} %get-tuple-element.6.rows_ref), custom_call_target="tpu_custom_call" | custom-call | tf_op jit(solution)/shard_map/pallas_call | solution.py:659
